TPU v7x, 256 devices: a whole 4x4x8 slice. The times are simulated.
256 devices in a mesh: ctx: 32 (over y, z), tp: 8 (over x, core).
Axes of the slice: x: 4, y: 4, z: 8, core: 2. Of those that a mesh axis runs over, the one named last changes fastest.
Arguments:
- context_block_rows: bfloat16 [16384, 8192], P('ctx', 'tp'), may hold values from -16 to 16
- query_hidden_rows: bfloat16 [64, 8192], P(None, 'tp'), may hold values from -16 to 16
- query_token_positions: int32 [64], replicated, may hold values from 16384 to 16573, as said below
- query_bound: int32 [64], replicated, may hold values from 1 to 16384, as said below
- query_matrix: bfloat16 [8192, 8192], P('ctx', 'tp'), may hold values from -0.0625 to 0.0625
- key_matrix: bfloat16 [8192, 1024], P('ctx', 'tp'), may hold values from -0.0625 to 0.0625
- value_matrix: bfloat16 [8192, 1024], P('ctx', 'tp'), may hold values from -0.0625 to 0.0625
Outputs:
- block_out: bfloat16 [16384, 8192], P('ctx', 'tp')
- query_out: bfloat16 [64, 8192], P(None, 'tp')
Inputs may be any that keep to these rules, and one draw needn't show every extreme that they name: query_token_positions rise strictly with the index; the first is 16384 and the last 16573. `query_bound`: some query token sees all 16384 context tokens.
All inputs are finite; a program needn't handle non-finite values.
Results may differ from a plain program's by a relative error of at most 0.0059.
The roundings to bfloat16 on the way count: a program that leaves them out, or rounds other values in their place, can miss the bound.
Values may be sent and summed in bfloat16 or wider, within the bound.
A program may use at most 128 MiB of HBM per device.

v0:
```python
import math
import jax
import jax.numpy as jnp
from jax import lax
from jax.sharding import PartitionSpec as P

HEAD_SIZE = 128


def from_root(value, axis, source):
    kept = jnp.where(lax.axis_index(axis) == source, value, 0).astype(value.dtype)
    return lax.psum(kept, axis)


def rope_table(half):
    values = []
    for index in range(half):
        freq = 500000.0 ** (-2.0 * index / (2.0 * half))
        wavelen = 2.0 * math.pi / freq
        if wavelen > 8192.0:
            values.append(freq / 8.0)
        elif wavelen < 2048.0:
            values.append(freq)
        else:
            smooth = (8192.0 / wavelen - 1.0) / 3.0
            values.append((1.0 - smooth) * freq / 8.0 + smooth * freq)
    return values


def apply_rotary(values, token_positions):
    half = values.shape[-1] // 2
    freqs = jnp.asarray(rope_table(half), jnp.float32)
    angle = token_positions.astype(jnp.float32)[:, None] * freqs[None, :]
    cosine = jnp.cos(angle)[:, None, :]
    sine = jnp.sin(angle)[:, None, :]
    first = values[..., :half]
    second = values[..., half:]
    return jnp.concatenate([first * cosine - second * sine, second * cosine + first * sine], -1)


def attend(query_heads_split, keys, values, valid):
    scale = 1.0 / math.sqrt(query_heads_split.shape[-1])
    scores = (
        jnp.einsum("qkgd,skd->qkgs", query_heads_split, keys, preferred_element_type=jnp.float32)
        * scale
    )
    scores = jnp.where(valid[:, None, None, :], scores, -1e30)
    peak = jnp.max(scores, -1)
    weights = jnp.exp(scores - peak[..., None])
    total = jnp.sum(weights, -1)
    mixed = jnp.einsum(
        "qkgs,skd->qkgd", weights.astype(jnp.bfloat16), values, preferred_element_type=jnp.float32
    )
    return (peak, total, mixed)


def on_device(
    context_block_rows,
    query_hidden_rows,
    query_token_positions,
    query_bound,
    query_matrix,
    key_matrix,
    value_matrix,
):
    ctx_index = lax.axis_index("ctx")
    blk = context_block_rows.shape[0]
    qcount = query_hidden_rows.shape[0]
    heads_q = query_matrix.shape[1] // HEAD_SIZE
    heads_kv = key_matrix.shape[1] // HEAD_SIZE
    head_group = heads_q // heads_kv
    whole_rows, whole_query = (
        lax.all_gather(context_block_rows, "tp", axis=1, tiled=True),
        lax.all_gather(query_hidden_rows, "tp", axis=1, tiled=True),
    )
    stacked = jnp.concatenate([whole_rows, whole_query], 0)
    head_rows = blk + qcount
    proj_query = jnp.dot(
        stacked,
        lax.all_gather(query_matrix, "ctx", axis=0, tiled=True),
        preferred_element_type=jnp.float32,
    )
    proj_key = jnp.dot(
        stacked,
        lax.all_gather(key_matrix, "ctx", axis=0, tiled=True),
        preferred_element_type=jnp.float32,
    )
    proj_value = jnp.dot(
        stacked,
        lax.all_gather(value_matrix, "ctx", axis=0, tiled=True),
        preferred_element_type=jnp.float32,
    )
    local_pos = ctx_index * blk + jnp.arange(blk, dtype=jnp.int32)
    k_block = apply_rotary(proj_key[:blk].reshape(blk, heads_kv, HEAD_SIZE), local_pos).astype(
        jnp.bfloat16
    )
    v_block = proj_value[:blk].reshape(blk, heads_kv, HEAD_SIZE).astype(jnp.bfloat16)
    key_token_rows = apply_rotary(
        proj_key[blk:head_rows].reshape(qcount, heads_kv, HEAD_SIZE), query_token_positions
    ).astype(jnp.bfloat16)
    value_token_rows = (
        proj_value[blk:head_rows].reshape(qcount, heads_kv, HEAD_SIZE).astype(jnp.bfloat16)
    )
    anchor_key, anchor_value = (from_root(k_block, "ctx", 0), from_root(v_block, "ctx", 0))
    q_block = apply_rotary(proj_query[:blk].reshape(blk, heads_q, HEAD_SIZE), local_pos).astype(
        jnp.bfloat16
    )
    query_token_rows = (
        apply_rotary(proj_query[blk:].reshape(qcount, heads_q, HEAD_SIZE), query_token_positions)
        .astype(jnp.bfloat16)
        .reshape(qcount, heads_kv, head_group, HEAD_SIZE)
    )
    keys_cat = jnp.concatenate([anchor_key, k_block], 0)
    values_cat = jnp.concatenate([anchor_value, v_block], 0)
    anchor_live = ctx_index > 0
    rows_step = min(blk, 512)
    rows_here = 0 + jnp.arange(rows_step, dtype=jnp.int32)
    valid = jnp.concatenate(
        [
            jnp.broadcast_to(anchor_live, (rows_step, blk)),
            rows_here[:, None] >= jnp.arange(blk, dtype=jnp.int32)[None, :],
        ],
        1,
    )
    query_heads_split = q_block.reshape(rows_step, heads_kv, head_group, HEAD_SIZE)
    peak, total, mixed = attend(query_heads_split, keys_cat, values_cat, valid)
    outputs = (
        (mixed / total[..., None]).astype(jnp.bfloat16).reshape(rows_step, heads_q * HEAD_SIZE)
    )
    valid_ctx = local_pos[None, :] < query_bound[:, None]
    peak, total, mixed = attend(query_token_rows, k_block, v_block, valid_ctx)
    top = lax.pmax(peak, "ctx")
    scaled = jnp.exp(peak - top)
    total_all, mixed_all = lax.psum((total * scaled, mixed * scaled[..., None]), "ctx")
    own = jnp.arange(qcount, dtype=jnp.int32)
    self_peak, self_total, self_mixed = attend(
        query_token_rows, key_token_rows, value_token_rows, own[:, None] >= own[None, :]
    )
    final = jnp.maximum(top, self_peak)
    w_ctx = jnp.exp(top - final)
    w_self = jnp.exp(self_peak - final)
    query_out = (mixed_all * w_ctx[..., None] + self_mixed * w_self[..., None]) / (
        total_all * w_ctx + self_total * w_self
    )[..., None]
    query_out = query_out.astype(jnp.bfloat16).reshape(qcount, heads_q * HEAD_SIZE)
    return (outputs, query_out)


def solution(mesh):
    placed = (
        P("ctx", "tp"),
        P(None, "tp"),
        P(),
        P(),
        P("ctx", "tp"),
        P("ctx", "tp"),
        P("ctx", "tp"),
    )
    return jax.shard_map(
        on_device,
        mesh=mesh,
        in_specs=placed,
        out_specs=(P("ctx", "tp"), P(None, "tp")),
        check_vma=False,
    )
```

profile of v0, /device:TPU:2, one launch (start us, length us, event | category | flops | bytes accessed | tf_op | source)
XLA Modules:
  0.0 689.7 jit_solution(3943614140132584248)
XLA Ops:
  11.3 0.9 concatenate.62
  12.3 1.4 broadcast_compare_fusion
  13.6 0.8 multiply_cosine_fusion.3
  14.5 2.5 multiply_cosine_fusion
  17.0 47.3 %all-gather.6.cloned.1.call-done = bf16[512,8192]{1,0:T(8,128)(2,1)} async-done(((bf16[512,1024]{1,0:T(8,128)(2,1)}), bf16[512,8192]{1,0:T(8,128)(2,1)}) %all-gather.6.cloned.1.call-update) | async-done | bytes 8388624 | tf_op jit(solution)/shard_map/all_gather | solution.py:73
  64.3 7.6 %constant_dynamic-update-slice_fusion.1 = bf16[576,8192]{1,0:T(8,128)(2,1)} fusion(bf16[512,8192]{1,0:T(8,128)(2,1)} %all-gather.6.cloned.1.call-done), kind=kLoop, calls=%fused_computation.100 | loop fusion | bytes 16777216
  71.9 19.5 %all-gather.8.cloned.1.call-done = bf16[64,8192]{1,0:T(8,128)(2,1)} async-done(((bf16[64,1024]{1,0:T(8,128)(2,1)}), bf16[64,8192]{1,0:T(8,128)(2,1)}) %all-gather.8.cloned.1.call-update) | async-done | bytes 1048592 | tf_op jit(solution)/shard_map/all_gather | solution.py:74
  91.4 2.3 constant_dynamic-update-slice_fusion
  93.7 79.8 %all-gather.12.cloned.1.call-done = bf16[8192,128]{1,0:T(8,128)(2,1)} async-done(((bf16[256,128]{1,0:T(8,128)(2,1)}), bf16[8192,128]{1,0:T(8,128)(2,1)}) %all-gather.12.cloned.1.call-update) | async-done | bytes 2097168 | tf_op jit(solution)/shard_map/all_gather | solution.py:85
  173.5 5.8 fusion.83
  179.4 1.2 fusion.35
  180.6 0.8 maximum_select_fusion
  181.4 0.8 fusion.64
  182.2 68.9 %all-gather.10.cloned.1.call-done = bf16[8192,128]{1,0:T(8,128)(2,1)} async-done(((bf16[256,128]{1,0:T(8,128)(2,1)}), bf16[8192,128]{1,0:T(8,128)(2,1)}) %all-gather.10.cloned.1.call-update) | async-done | bytes 2097168 | tf_op jit(solution)/shard_map/all_gather | solution.py:90
  251.1 6.9 convolution_convert_fusion
  258.0 0.7 slice_bitcast_fusion.3
  258.9 132.5 %all-gather.14.cloned.1.call-done = bf16[8192,1024]{1,0:T(8,128)(2,1)} async-done(((bf16[256,1024]{1,0:T(8,128)(2,1)}), bf16[8192,1024]{1,0:T(8,128)(2,1)}) %all-gather.14.cloned.1.call-update) | async-done | bytes 16777232 | tf_op jit(solution)/shard_map/all_gather | solution.py:80
  391.4 14.9 %fusion.84 = f32[576,1024]{1,0:T(8,128)S(1)} fusion(bf16[576,8192]{1,0:T(8,128)(2,1)} %constant_dynamic-update-slice_fusion, bf16[8192,1024]{1,0:T(8,128)(2,1)} %all-gather.14.cloned.1.call-done), kind=kOutput, calls=%fused_computation.126 | convolution fusion | flops 9663676416 | bytes 28573696 | tf_op jit(solution)/shard_map/dot_general | solution.py:78
  406.8 1.4 fusion.81
  408.2 1.0 fusion.25
  409.1 71.4 %pmax.7 = f32[64,1,8]{0,2,1:T(8,128)S(1)} all-reduce(f32[64,1,8]{0,2,1:T(8,128)S(1)} %bitcast.169), channel_id=1, replica_groups=mesh['ctx'=32,'tp'=8] {'ctx'}, use_global_device_ids=true, to_apply=%region_5.6 | all-reduce | flops 512 | bytes 4096 | tf_op jit(solution)/shard_map/pmax | solution.py:132
  481.1 2.0 fusion.79
  483.7 1.1 fusion.14
  484.8 3.5 subtract_convert_fusion
  488.2 47.8 %all-reduce.7.cloned.1.call-done = (bf16[512,1,128]{2,0,1:T(8,128)(2,1)}, bf16[512,1,128]{2,0,1:T(8,128)(2,1)}) async-done(((bf16[512,1,128]{2,0,1:T(8,128)(2,1)}, bf16[512,1,128]{2,0,1:T(8,128)(2,1)}), (bf16[512,1,128]{2,0,1:T(8,128)(2,1)}, bf16[512,1,128]{2,0,1:T(8,128)(2,1)})) %all-reduce.7.cloned.1.call-update) | async-done | bytes 262160 | tf_op jit(solution)/shard_map/psum | solution.py:12
  536.1 10.7 %fusion.2 = (f32[512,8]{0,1:T(8,128)S(1)}, f32[1024,512,8]{1,0,2:T(8,128)}) fusion(pred[512,1024]{0,1:T(8,128)(4,1)} %concatenate.62, bf16[512,8,64]{2,0,1:T(8,128)(2,1)} %get-tuple-element.9, bf16[512,8,64]{2,0,1:T(8,128)(2,1)S(1)} %get-tuple-element.8, bf16[512,1,64]{2,0,1:T(8,128)(2,1)} %copy-done.1, bf16[512,1,64]{2,0,1:T(8,128)(2,1)S(1)} %get-tuple-element.14, ...), kind=kOutput, calls=%fused_computation.4 | convolution fusion | flops 1089204224 | bytes 18628608 | tf_op jit(solution)/shard_map/qkgd,skd->qkgs/dot_general | solution.py:44
  546.8 9.3 %fusion = f32[512,8]{0,1:T(8,128)S(1)} fusion(f32[1024,512,8]{1,0,2:T(8,128)} %get-tuple-element.32, f32[512,8]{0,1:T(8,128)S(1)} %get-tuple-element.31, pred[512,1024]{0,1:T(8,128)(4,1)S(1)} %copy-done), kind=kLoop, calls=%fused_computation.2 | loop fusion | flops 16773120 | bytes 17334272 | tf_op jit(solution)/shard_map/reduce_sum | solution.py:50
  556.5 9.1 %fusion.7 = bf16[1,128,512,8]{2,1,3,0:T(8,128)(2,1)S(1)} fusion(f32[1024,512,8]{1,0,2:T(8,128)} %get-tuple-element.32, f32[512,8]{0,1:T(8,128)S(1)} %get-tuple-element.31, pred[512,1024]{0,1:T(8,128)(4,1)S(1)} %copy-done, f32[512,8]{0,1:T(8,128)S(1)} %fusion, bf16[512,1,128]{2,0,1:T(8,128)(2,1)S(1)} %copy-done.4, bf16[512,1,128]{2,0,1:T(8,128)(2,1)S(1)} %copy-done.10), kind=kOutput, calls=%fused_computation.10 | convolution fusion | flops 1092091904 | bytes 18644992 | tf_op jit(solution)/shard_map/qkgs,skd->qkgd/dot_general | solution.py:51
  565.7 1.3 copy.29
  567.0 72.5 %psum.31 = f32[64,1,8]{0,2,1:T(8,128)S(1)} all-reduce(f32[64,1,8]{0,2,1:T(8,128)S(1)} %copy-done.8), channel_id=1, replica_groups=mesh['ctx'=32,'tp'=8] {'ctx'}, use_global_device_ids=true, to_apply=%region_9.10 | all-reduce | flops 512 | bytes 4096 | tf_op jit(solution)/shard_map/psum | solution.py:134
  639.5 41.2 %all-reduce.5.cloned.1.call-done = f32[64,1,8,128]{3,0,2,1:T(8,128)} async-done(((f32[64,1,8,128]{3,0,2,1:T(8,128)}), f32[64,1,8,128]{3,0,2,1:T(8,128)}) %all-reduce.5.cloned.1.call-update) | async-done | bytes 262160 | tf_op jit(solution)/shard_map/psum | solution.py:134
  680.7 1.3 fusion.19
  (55 shorter events, 6.9 us)
Async XLA Ops:
  7.2 57.1 %all-gather.6.cloned.1.call-start = ((), (), s32[]{:S(2)}) async-start(), calls=%async_computation | async-start | bytes 9437184 | tf_op jit(solution)/shard_map/all_gather | solution.py:73
  7.9 83.5 %all-gather.8.cloned.1.call-start = ((), (), s32[]{:S(2)}) async-start(), calls=%async_computation.1 | async-start | bytes 1179648 | tf_op jit(solution)/shard_map/all_gather | solution.py:74
  8.6 164.9 %all-gather.12.cloned.1.call-start = ((), (), s32[]{:S(2)}) async-start(), calls=%async_computation.3 | async-start | bytes 2162688 | tf_op jit(solution)/shard_map/all_gather | solution.py:85
  9.4 241.7 %all-gather.10.cloned.1.call-start = ((), (), s32[]{:S(2)}) async-start(), calls=%async_computation.2 | async-start | bytes 2162688 | tf_op jit(solution)/shard_map/all_gather | solution.py:90
  10.0 381.4 %all-gather.14.cloned.1.call-start = ((), (), s32[]{:S(2)}) async-start(), calls=%async_computation.4 | async-start | bytes 17301504 | tf_op jit(solution)/shard_map/all_gather | solution.py:80
  10.5 525.5 %all-reduce.7.cloned.1.call-start = ((), (), s32[]{:S(2)}) async-start(), calls=%async_computation.6 | async-start | bytes 524288 | tf_op jit(solution)/shard_map/psum | solution.py:12
  71.9 107.5 %copy-start.9 = (f32[64]{0:T(128)S(1)}, f32[64]{0:T(128)}, u32[]{:S(2)}) copy-start(f32[64]{0:T(128)} %constant.24.clone) | copy-start | bytes 772
  180.6 225.7 %copy-start.1 = (bf16[512,1,64]{2,0,1:T(8,128)(2,1)}, bf16[512,1,64]{2,0,1:T(8,128)(2,1)S(1)}, u32[]{:S(2)}) copy-start(bf16[512,1,64]{2,0,1:T(8,128)(2,1)S(1)} %get-tuple-element.15) | copy-start | bytes 196612
  258.0 133.4 %copy-start.2 = (bf16[576,128]{1,0:T(8,128)(2,1)}, bf16[576,128]{1,0:T(8,128)(2,1)S(1)}, u32[]{:S(2)}) copy-start(bf16[576,128]{1,0:T(8,128)(2,1)S(1)} %convolution_convert_fusion) | copy-start | bytes 442372
  258.8 421.9 %all-reduce.5.cloned.1.call-start = ((), (), s32[]{:S(2)}) async-start(), calls=%async_computation.5 | async-start | bytes 524288 | tf_op jit(solution)/shard_map/psum | solution.py:134
  480.6 2.5 copy-start.7
  480.6 3.1 copy-start.3
  536.1 10.7 %copy-start = (pred[512,1024]{0,1:T(8,128)(4,1)S(1)}, pred[512,1024]{0,1:T(8,128)(4,1)}, u32[]{:S(2)}) copy-start(pred[512,1024]{0,1:T(8,128)(4,1)} %concatenate.62) | copy-start | bytes 1572868
  546.8 9.3 %copy-start.5 = (bf16[64,64]{1,0:T(8,128)(2,1)S(1)}, bf16[64,64]{1,0:T(8,128)(2,1)}, u32[]{:S(2)}) copy-start(bf16[64,64]{1,0:T(8,128)(2,1)} %get-tuple-element.20) | copy-start | bytes 24580
  546.8 9.3 %copy-start.6 = (bf16[64,64]{1,0:T(8,128)(2,1)S(1)}, bf16[64,64]{1,0:T(8,128)(2,1)}, u32[]{:S(2)}) copy-start(bf16[64,64]{1,0:T(8,128)(2,1)} %get-tuple-element.21) | copy-start | bytes 24580
  546.8 9.6 %copy-start.4 = (bf16[512,1,128]{2,0,1:T(8,128)(2,1)S(1)}, bf16[512,1,128]{2,0,1:T(8,128)(2,1)}, u32[]{:S(2)}) copy-start(bf16[512,1,128]{2,0,1:T(8,128)(2,1)} %get-tuple-element.18) | copy-start | bytes 393220
  546.8 9.6 %copy-start.10 = (bf16[512,1,128]{2,0,1:T(8,128)(2,1)S(1)}, bf16[512,1,128]{2,0,1:T(8,128)(2,1)}, u32[]{:S(2)}) copy-start(bf16[512,1,128]{2,0,1:T(8,128)(2,1)} %get-tuple-element.7) | copy-start | bytes 393220
  556.5 10.5 %copy-start.8 = (f32[64,1,8]{0,2,1:T(8,128)S(1)}, f32[64,1,8]{0,2,1:T(8,128)}, u32[]{:S(2)}) copy-start(f32[64,1,8]{0,2,1:T(8,128)} %get-tuple-element.25) | copy-start | bytes 6148
Sparse Core Ops, SparseCore 0:
  9.8 54.4 all-gather.5
  66.1 25.2 all-gather.7
  94.0 79.4 all-gather.11
  176.0 75.1 all-gather.9
  253.6 137.7 all-gather.13
  394.7 141.2 all-reduce.6
  539.5 141.1 all-reduce.4
where the time goes:
time: 690 us
  waiting for transfers between devices  440 us (64%)
  blocking collectives  144 us (21%)
  matrix products  51.5 us (7%)
  other arithmetic  23.5 us (3%)
  local copies, waits for them, and re-layouts  15.8 us (2%)
  between operations  14.4 us (2%)
    all_gather x1, waiting for transfers between devices, on_device(): lax.all_gather(query_matrix, 'ctx', axis=0, tiled=True)  133 us
    all_gather x1, waiting for transfers between devices, on_device(): lax.all_gather(key_matrix, 'ctx', axis=0, tiled=True)  79.8 us
    psum x1, blocking collectives, on_device(): lax.psum((total * scaled, mixed * scaled[..., None]), 'ctx')  72.5 us
    pmax x1, blocking collectives, on_device(): top = lax.pmax(peak, 'ctx')  71.4 us
    all_gather x1, waiting for transfers between devices, on_device(): lax.all_gather(value_matrix, 'ctx', axis=0, tiled=True)  68.9 us
    psum x1, waiting for transfers between devices, from_root(): return lax.psum(kept, axis)  47.8 us
    all_gather x1, waiting for transfers between devices, on_device(): lax.all_gather(context_block_rows, 'tp', axis=1, tiled=True)  47.3 us
    psum x1, waiting for transfers between devices, on_device(): lax.psum((total * scaled, mixed * scaled[..., None]), 'ctx')  41.2 us
  transfers between devices with their start and end apart: 7, of which 7 were waited for; matrix products, arithmetic and copies ran while one was open for 13% of the time, Pallas kernels for 0%

commit v1 on v0

--- a/solution.py
+++ b/solution.py
@@ -7,9 +7,13 @@
 HEAD_SIZE = 128
 
 
+def case_take(net_axis, local):
+    return jnp.sum(lax.all_gather(local, net_axis), 0)
+
+
 def from_root(value, axis, source):
     kept = jnp.where(lax.axis_index(axis) == source, value, 0).astype(value.dtype)
-    return lax.psum(kept, axis)
+    return case_take(axis, kept)
 
 
 def rope_table(half):

time: 690 us -> 794 us (1.15)
  waiting for transfers between devices: 440 us -> 547 us
    all_gather x0 -> x2, waiting for transfers between devices: none -> 146 us  [case_take(): return jnp.sum(lax.all_gather(local, net_axis), 0)]
    psum x1 -> x0, waiting for transfers between devices: 47.8 us -> none  [from_root(): return lax.psum(kept, axis)]
    all_gather x1, waiting for transfers between devices: 68.9 us -> 79.8 us  [on_device(): lax.all_gather(value_matrix, 'ctx', axis=0, tiled=True)]
    all_gather x1, waiting for transfers between devices: 79.8 us -> 69.2 us  [on_device(): lax.all_gather(key_matrix, 'ctx', axis=0, tiled=True)]
  transfers between devices with their start and end apart: 7 -> 8, of which waited for: 7 -> 8; matrix products, arithmetic and copies ran while one was open for 13% -> 8% of each run, Pallas kernels for 0% -> 0%
where the time goes in v1:
time: 794 us
  waiting for transfers between devices  547 us (69%)
  blocking collectives  141 us (18%)
  matrix products  49.2 us (6%)
  other arithmetic  25.7 us (3%)
  local copies, waits for them, and re-layouts  15.1 us (2%)
  between operations  14.5 us (2%)
    all_gather x2, waiting for transfers between devices, case_take(): return jnp.sum(lax.all_gather(local, net_axis), 0)  146 us
    all_gather x1, waiting for transfers between devices, on_device(): lax.all_gather(query_matrix, 'ctx', axis=0, tiled=True)  137 us
    all_gather x1, waiting for transfers between devices, on_device(): lax.all_gather(value_matrix, 'ctx', axis=0, tiled=True)  79.8 us
    pmax x1, blocking collectives, on_device(): top = lax.pmax(peak, 'ctx')  71.4 us
    psum x1, blocking collectives, on_device(): lax.psum((total * scaled, mixed * scaled[..., None]), 'ctx')  70.1 us
    all_gather x1, waiting for transfers between devices, on_device(): lax.all_gather(key_matrix, 'ctx', axis=0, tiled=True)  69.2 us
    all_gather x1, waiting for transfers between devices, on_device(): lax.all_gather(context_block_rows, 'tp', axis=1, tiled=True)  54.3 us
    psum x1, waiting for transfers between devices, on_device(): lax.psum((total * scaled, mixed * scaled[..., None]), 'ctx')  38.3 us
  transfers between devices with their start and end apart: 8, of which 8 were waited for; matrix products, arithmetic and copies ran while one was open for 8% of the time, Pallas kernels for 0%

profile of v1, /device:TPU:2, one launch (start us, length us, event | category | flops | bytes accessed | tf_op | source)
XLA Modules:
  0.0 793.9 jit_solution(241551781261374322)
XLA Ops:
  10.0 54.3 %all-gather.9.cloned.1.call-done = bf16[512,8192]{1,0:T(8,128)(2,1)} async-done(((bf16[512,1024]{1,0:T(8,128)(2,1)}), bf16[512,8192]{1,0:T(8,128)(2,1)}) %all-gather.9.cloned.1.call-update) | async-done | bytes 8388624 | tf_op jit(solution)/shard_map/all_gather | solution.py:77
  64.3 7.6 constant_dynamic-update-slice_fusion.1
  71.9 19.5 %all-gather.11.cloned.1.call-done = bf16[64,8192]{1,0:T(8,128)(2,1)} async-done(((bf16[64,1024]{1,0:T(8,128)(2,1)}), bf16[64,8192]{1,0:T(8,128)(2,1)}) %all-gather.11.cloned.1.call-update) | async-done | bytes 1048592 | tf_op jit(solution)/shard_map/all_gather | solution.py:78
  91.4 2.4 constant_dynamic-update-slice_fusion
  93.7 79.8 %all-gather.13.cloned.1.call-done = bf16[8192,128]{1,0:T(8,128)(2,1)} async-done(((bf16[256,128]{1,0:T(8,128)(2,1)}), bf16[8192,128]{1,0:T(8,128)(2,1)}) %all-gather.13.cloned.1.call-update) | async-done | bytes 2097168 | tf_op jit(solution)/shard_map/all_gather | solution.py:94
  173.5 7.0 convolution_convert_fusion
  181.9 69.2 %all-gather.15.cloned.1.call-done = bf16[8192,128]{1,0:T(8,128)(2,1)} async-done(((bf16[256,128]{1,0:T(8,128)(2,1)}), bf16[8192,128]{1,0:T(8,128)(2,1)}) %all-gather.15.cloned.1.call-update) | async-done | bytes 2097168 | tf_op jit(solution)/shard_map/all_gather | solution.py:89
  251.1 5.8 fusion.83
  257.0 1.2 fusion.35
  258.2 0.8 maximum_select_fusion
  260.1 0.9 concatenate.73
  261.9 1.8 multiply_cosine_fusion
  263.7 0.8 fusion.64
  264.5 68.1 %all-gather.21.cloned.1.call-done = bf16[16384,128]{1,0:T(8,128)(2,1)} async-done(((bf16[512,128]{1,0:T(8,128)(2,1)}), bf16[16384,128]{1,0:T(8,128)(2,1)}) %all-gather.21.cloned.1.call-update) | async-done | bytes 4194320 | tf_op jit(solution)/shard_map/all_gather | solution.py:11
  332.6 3.5 reduce.10
  336.1 78.1 %all-gather.17.cloned.1.call-done = bf16[32,512,1,128]{3,1,2,0:T(8,128)(2,1)} async-done(((bf16[1,512,1,128]{3,1,2,0:T(8,128)(2,1)}), bf16[32,512,1,128]{3,1,2,0:T(8,128)(2,1)}) %all-gather.17.cloned.1.call-update) | async-done | bytes 4194320 | tf_op jit(solution)/shard_map/all_gather | solution.py:11
  414.1 3.4 reduce_sum.61
  417.6 137.0 %all-gather.19.cloned.1.call-done = bf16[8192,1024]{1,0:T(8,128)(2,1)} async-done(((bf16[256,1024]{1,0:T(8,128)(2,1)}), bf16[8192,1024]{1,0:T(8,128)(2,1)}) %all-gather.19.cloned.1.call-update) | async-done | bytes 16777232 | tf_op jit(solution)/shard_map/all_gather | solution.py:84
  554.6 14.9 %fusion.84 = f32[576,1024]{1,0:T(8,128)S(1)} fusion(bf16[576,8192]{1,0:T(8,128)(2,1)} %constant_dynamic-update-slice_fusion, bf16[8192,1024]{1,0:T(8,128)(2,1)} %all-gather.19.cloned.1.call-done), kind=kOutput, calls=%fused_computation.126 | convolution fusion | flops 9663676416 | bytes 28573696 | tf_op jit(solution)/shard_map/dot_general | solution.py:82
  570.0 1.4 fusion.81
  571.4 0.9 fusion.25
  572.3 71.4 %pmax.7 = f32[64,1,8]{0,2,1:T(8,128)S(1)} all-reduce(f32[64,1,8]{0,2,1:T(8,128)S(1)} %bitcast.177), channel_id=1, replica_groups=mesh['ctx'=32,'tp'=8] {'ctx'}, use_global_device_ids=true, to_apply=%region_5.6 | all-reduce | flops 512 | bytes 4096 | tf_op jit(solution)/shard_map/pmax | solution.py:136
  643.8 1.3 bitcast_multiply_fusion.1
  645.0 2.0 fusion.14
  648.2 0.8 subtract_convert_fusion
  649.1 7.6 fusion.2
  656.7 9.3 %fusion = f32[512,8]{0,1:T(8,128)S(1)} fusion(f32[1024,512,8]{1,0,2:T(8,128)} %get-tuple-element.32, f32[512,8]{0,1:T(8,128)S(1)} %get-tuple-element.31, pred[512,1024]{0,1:T(8,128)(4,1)S(1)} %copy-done), kind=kLoop, calls=%fused_computation.2 | loop fusion | flops 16773120 | bytes 17334272 | tf_op jit(solution)/shard_map/reduce_sum | solution.py:54
  666.4 8.9 %fusion.7 = bf16[1,128,512,8]{2,1,3,0:T(8,128)(2,1)S(1)} fusion(f32[1024,512,8]{1,0,2:T(8,128)} %get-tuple-element.32, f32[512,8]{0,1:T(8,128)S(1)} %get-tuple-element.31, pred[512,1024]{0,1:T(8,128)(4,1)S(1)} %copy-done, f32[512,8]{0,1:T(8,128)S(1)} %fusion, bf16[512,1,128]{2,0,1:T(8,128)(2,1)S(1)} %copy-done.9, bf16[512,1,128]{2,0,1:T(8,128)(2,1)S(1)} %bitcast.174), kind=kOutput, calls=%fused_computation.10 | convolution fusion | flops 1092091904 | bytes 18644992 | tf_op jit(solution)/shard_map/qkgs,skd->qkgd/dot_general | solution.py:55
  675.3 1.3 copy.38
  676.6 70.1 %psum.15 = f32[64,1,8]{0,2,1:T(8,128)S(1)} all-reduce(f32[64,1,8]{0,2,1:T(8,128)S(1)} %copy-done.12), channel_id=1, replica_groups=mesh['ctx'=32,'tp'=8] {'ctx'}, use_global_device_ids=true, to_apply=%region_9.10 | all-reduce | flops 512 | bytes 4096 | tf_op jit(solution)/shard_map/psum | solution.py:138
  746.7 38.3 %all-reduce.3.cloned.1.call-done = f32[64,1,8,128]{3,0,2,1:T(8,128)} async-done(((f32[64,1,8,128]{3,0,2,1:T(8,128)}), f32[64,1,8,128]{3,0,2,1:T(8,128)}) %all-reduce.3.cloned.1.call-update) | async-done | bytes 262160 | tf_op jit(solution)/shard_map/psum | solution.py:138
  785.0 1.3 fusion.19
  (70 shorter events, 9.0 us)
Async XLA Ops:
  7.2 57.1 %all-gather.9.cloned.1.call-start = ((), (), s32[]{:S(2)}) async-start(), calls=%async_computation | async-start | bytes 9437184 | tf_op jit(solution)/shard_map/all_gather | solution.py:77
  7.9 83.5 %all-gather.11.cloned.1.call-start = ((), (), s32[]{:S(2)}) async-start(), calls=%async_computation.1 | async-start | bytes 1179648 | tf_op jit(solution)/shard_map/all_gather | solution.py:78
  8.6 164.9 %all-gather.13.cloned.1.call-start = ((), (), s32[]{:S(2)}) async-start(), calls=%async_computation.2 | async-start | bytes 2162688 | tf_op jit(solution)/shard_map/all_gather | solution.py:94
  9.4 241.7 %all-gather.15.cloned.1.call-start = ((), (), s32[]{:S(2)}) async-start(), calls=%async_computation.3 | async-start | bytes 2162688 | tf_op jit(solution)/shard_map/all_gather | solution.py:89
  10.0 322.7 %all-gather.21.cloned.1.call-start = ((), (), s32[]{:S(2)}) async-start(), calls=%async_computation.7 | async-start | bytes 4325376 | tf_op jit(solution)/shard_map/all_gather | solution.py:11
  180.5 0.7 copy-start.5
  181.1 75.8 %copy-start.13 = (f32[64]{0:T(128)S(1)}, f32[64]{0:T(128)}, u32[]{:S(2)}) copy-start(f32[64]{0:T(128)} %constant.26.clone) | copy-start | bytes 772
  181.1 78.9 %copy-start.15 = (s32[64]{0:T(128)S(1)}, s32[64]{0:T(128)}, u32[]{:S(2)}) copy-start(s32[64]{0:T(128)} %param.13) | copy-start | bytes 772
  181.9 79.1 %copy-start.14 = (s32[64]{0:T(128)S(1)}, s32[64]{0:T(128)}, u32[]{:S(2)}) copy-start(s32[64]{0:T(128)} %param.14) | copy-start | bytes 772
  181.9 232.2 %all-gather.17.cloned.1.call-start = ((), (), s32[]{:S(2)}) async-start(), calls=%async_computation.4 | async-start | bytes 4325376 | tf_op jit(solution)/shard_map/all_gather | solution.py:11
  258.2 311.3 %copy-start.1 = (bf16[512,1,64]{2,0,1:T(8,128)(2,1)}, bf16[512,1,64]{2,0,1:T(8,128)(2,1)S(1)}, u32[]{:S(2)}) copy-start(bf16[512,1,64]{2,0,1:T(8,128)(2,1)S(1)} %get-tuple-element.15) | copy-start | bytes 196612
  259.0 295.6 %all-gather.19.cloned.1.call-start = ((), (), s32[]{:S(2)}) async-start(), calls=%async_computation.5 | async-start | bytes 17301504 | tf_op jit(solution)/shard_map/all_gather | solution.py:84
  259.8 525.2 %all-reduce.3.cloned.1.call-start = ((), (), s32[]{:S(2)}) async-start(), calls=%async_computation.6 | async-start | bytes 524288 | tf_op jit(solution)/shard_map/psum | solution.py:138
  554.6 15.4 %copy-start.8 = (pred[64,512]{1,0:T(8,128)(4,1)S(1)}, pred[64,512]{1,0:T(8,128)(4,1)}, u32[]{:S(2)}) copy-start(pred[64,512]{1,0:T(8,128)(4,1)} %broadcast_compare_fusion) | copy-start | bytes 98308
  647.0 1.2 copy-start.3
  647.0 1.2 copy-start.4
  647.5 1.5 copy-start
  647.5 1.5 copy-start.2
  647.5 1.5 copy-start.7
  656.7 9.3 %copy-start.10 = (bf16[64,64]{1,0:T(8,128)(2,1)S(1)}, bf16[64,64]{1,0:T(8,128)(2,1)}, u32[]{:S(2)}) copy-start(bf16[64,64]{1,0:T(8,128)(2,1)} %get-tuple-element.20) | copy-start | bytes 24580
  656.7 9.3 %copy-start.11 = (bf16[64,64]{1,0:T(8,128)(2,1)S(1)}, bf16[64,64]{1,0:T(8,128)(2,1)}, u32[]{:S(2)}) copy-start(bf16[64,64]{1,0:T(8,128)(2,1)} %get-tuple-element.21) | copy-start | bytes 24580
  656.7 9.6 %copy-start.6 = (bf16[512,128]{1,0:T(8,128)(2,1)S(1)}, bf16[512,128]{1,0:T(8,128)(2,1)}, u32[]{:S(2)}) copy-start(bf16[512,128]{1,0:T(8,128)(2,1)} %reduce.10) | copy-start | bytes 393220
  656.7 9.6 %copy-start.9 = (bf16[512,1,128]{2,0,1:T(8,128)(2,1)S(1)}, bf16[512,1,128]{2,0,1:T(8,128)(2,1)}, u32[]{:S(2)}) copy-start(bf16[512,1,128]{2,0,1:T(8,128)(2,1)} %get-tuple-element.19) | copy-start | bytes 393220
  666.4 10.3 %copy-start.12 = (f32[64,1,8]{0,2,1:T(8,128)S(1)}, f32[64,1,8]{0,2,1:T(8,128)}, u32[]{:S(2)}) copy-start(f32[64,1,8]{0,2,1:T(8,128)} %get-tuple-element.25) | copy-start | bytes 6148
Sparse Core Ops, SparseCore 0:
  9.8 54.4 all-gather.8
  66.1 25.2 all-gather.10
  94.0 79.4 all-gather.12
  175.9 75.1 all-gather.14
  253.6 79.0 all-gather.20
  335.1 79.0 all-gather.16
  416.7 137.8 all-gather.18
  647.2 137.8 all-reduce.2
